TPU v7x, 256 devices: a whole 4x4x8 slice. The times are simulated.
256 devices in a mesh: blk: 8 (over z_lo, x), head: 32 (over y, z_hi, core).
Axes of the slice: x: 4, y: 4, z: 8 (z_hi: 4, z_lo: 2; z = z_hi * 2 + z_lo), core: 2. Of those that a mesh axis runs over, the one named last changes fastest.
Arguments:
- query_rows: bfloat16 [32768, 4096], P(('blk', 'head')), may hold values from -12 to 12
- key_rows: bfloat16 [32768, 4096], P(('blk', 'head')), may hold values from -12 to 12
- value_rows: bfloat16 [32768, 4096], P(('blk', 'head')), may hold values from -6 to 6
- block_lists: int32 [32, 256, 16], P('head', 'blk'), may hold values from 0 to 255, as said below
Outputs:
- mixed: bfloat16 [32768, 4096], P(('blk', 'head'))
Inputs may be any that keep to these rules, and one draw needn't show every extreme that they name: Each row block_lists[h, i, :] names 16 distinct key blocks in ascending order; they may lie anywhere in the clip.
All inputs are finite; a program needn't handle non-finite values.
Results may differ from a plain program's by a relative error of at most 0.007.
Values may be sent and summed in bfloat16 or wider, within the bound.
A program may use at most 128 MiB of HBM per device.

v0:
```python
import jax
import jax.numpy as jnp
from jax import lax
from jax.sharding import PartitionSpec as P

BLOCK = 128


NEGATIVE = -1e30


def absorb(carry_state, query_blocks, key_piece, value_piece, head_lists, first_block):
    block_rows = query_blocks.shape[1]
    head_dim = query_blocks.shape[2]
    piece_blocks = key_piece.shape[0] // block_rows
    key_blocks = key_piece.reshape(piece_blocks, block_rows, head_dim)
    value_blocks = value_piece.reshape(piece_blocks, block_rows, head_dim)
    live_width = head_lists.shape[1]
    width_sub = min(live_width, 8)
    in_piece = (head_lists >= first_block) & (head_lists < first_block + piece_blocks)
    lower_bound = jnp.sum((head_lists < first_block).astype(jnp.int32), axis=1)
    live_count = jnp.sum(in_piece.astype(jnp.int32), axis=1)
    rounds = (jnp.max(live_count) + width_sub - 1) // width_sub
    offsets = jnp.arange(width_sub, dtype=jnp.int32)
    score_scale = head_dim ** (-0.5)

    def one_turn(turn_index, inner):
        running_max, running_sum, running_acc = inner
        position = turn_index * width_sub + offsets
        usable = position[None, :] < live_count[:, None]
        gather_index = jnp.clip(lower_bound[:, None] + position[None, :], 0, live_width - 1)
        entries = jnp.take_along_axis(head_lists, gather_index, axis=1)
        relative = jnp.clip(entries, 0, piece_blocks - 1)
        picked_keys = key_blocks[relative]
        picked_values = value_blocks[relative]
        scores = (
            jnp.einsum(
                "qtd,qskd->qtsk", query_blocks, picked_keys, preferred_element_type=jnp.float32
            )
            * score_scale
        )
        usable_mask = usable[:, None, :, None]
        scores = jnp.where(usable_mask, scores, NEGATIVE)
        new_max = jnp.maximum(running_max, jnp.max(scores, axis=(2, 3)))
        weights = jnp.where(usable_mask, jnp.exp(scores - new_max[:, :, None, None]), 0.0)
        factor = jnp.exp(running_max - new_max)
        running_sum = running_sum * factor + jnp.sum(weights, axis=(2, 3))
        added = jnp.einsum(
            "qtsk,qskd->qtd",
            weights.astype(jnp.bfloat16),
            picked_values,
            preferred_element_type=jnp.float32,
        )
        running_acc = running_acc * factor[:, :, None] + added
        return (new_max, running_sum, running_acc)

    return lax.fori_loop(0, rounds, one_turn, carry_state)


def on_device(query_rows, key_rows, value_rows, block_lists):
    query_local, key_local, value_local = (
        lax.all_to_all(query_rows, "head", split_axis=1, concat_axis=0, tiled=True),
        lax.all_to_all(key_rows, "head", split_axis=1, concat_axis=0, tiled=True),
        lax.all_to_all(value_rows, "head", split_axis=1, concat_axis=0, tiled=True),
    )
    local_rows, local_width = query_local.shape
    heads_here = block_lists.shape[0]
    head_dim = local_width // heads_here
    block_count = local_rows // BLOCK

    def head_query():
        return query_local.reshape(block_count, BLOCK, head_dim)

    initial = tuple(
        (
            (
                jnp.full((block_count, BLOCK), NEGATIVE, jnp.float32),
                jnp.zeros((block_count, BLOCK), jnp.float32),
                jnp.zeros((block_count, BLOCK, head_dim), jnp.float32),
            )
            for head_number in range(heads_here)
        )
    )
    key_whole, value_whole = (
        lax.all_gather(key_local, "blk", axis=0, tiled=True),
        lax.all_gather(value_local, "blk", axis=0, tiled=True),
    )
    first_block = jnp.int32(0)
    finals = tuple(
        (
            absorb(
                initial[head_number],
                head_query(),
                key_whole,
                value_whole,
                block_lists[head_number],
                first_block,
            )
            for head_number in range(heads_here)
        )
    )
    outputs = [
        (accumulated / total_sum[:, :, None]).reshape(local_rows, head_dim)
        for peak_value, total_sum, accumulated in finals
    ]
    blended = outputs[0].astype(jnp.bfloat16)
    return lax.all_to_all(blended, "head", split_axis=0, concat_axis=1, tiled=True)


def solution(mesh):
    in_specs = (
        P(("blk", "head"), None),
        P(("blk", "head"), None),
        P(("blk", "head"), None),
        P("head", "blk", None),
    )
    out_specs = P(("blk", "head"), None)
    return jax.shard_map(
        on_device, mesh=mesh, in_specs=in_specs, out_specs=out_specs, check_vma=False
    )
```

profile of v0, /device:TPU:1, one launch (start us, length us, event | category | flops | bytes accessed | tf_op | source)
XLA Modules:
  0.0 422.4 jit_solution(6896183586989585161)
XLA Ops:
  6.5 1.7 copy.23
  8.3 0.7 copy.24
  8.9 41.6 %all_to_all.70 = bf16[128,32,128]{2,0,1:T(8,128)(2,1)} all-to-all(bf16[128,32,128]{2,0,1:T(8,128)(2,1)S(1)} %copy.24), channel_id=1, replica_groups=mesh['blk'=8,'head'=32] {'head'}, dimensions={1} | all-to-all | bytes 2097152 | tf_op jit(solution)/shard_map/all_to_all | solution.py:64
  50.6 1.6 copy.20
  52.2 0.7 copy.21
  52.9 45.7 %all_to_all.71 = bf16[128,32,128]{2,0,1:T(8,128)(2,1)} all-to-all(bf16[128,32,128]{2,0,1:T(8,128)(2,1)S(1)} %copy.21), channel_id=1, replica_groups=mesh['blk'=8,'head'=32] {'head'}, dimensions={1} | all-to-all | bytes 2097152 | tf_op jit(solution)/shard_map/all_to_all | solution.py:63
  98.6 1.3 copy.22
  99.9 5.0 %all-to-all-start.1 = ((bf16[128,32,128]{0,2,1:T(8,128)(2,1)}), bf16[128,32,128]{0,2,1:T(8,128)(2,1)S(1)}, u32[]{:S(2)}, u32[]{:S(2)}) async-start(bf16[128,32,128]{0,2,1:T(8,128)(2,1)} %bitcast.5), calls=%async_computation.1 | async-start | bytes 2097152 | tf_op jit(solution)/shard_map/all_to_all | solution.py:62
  104.9 0.7 reduce_max.18
  106.2 39.6 %all-to-all-done.1 = bf16[128,32,128]{0,2,1:T(8,128)(2,1)S(1)} async-done(((bf16[128,32,128]{0,2,1:T(8,128)(2,1)}), bf16[128,32,128]{0,2,1:T(8,128)(2,1)S(1)}, u32[]{:S(2)}, u32[]{:S(2)}) %all-to-all-start.1) | async-done | bytes 1048608 | tf_op jit(solution)/shard_map/all_to_all | solution.py:62
  145.8 0.7 copy.25
  146.5 39.3 %all-gather.5.cloned.1.call-done = bf16[32768,128]{1,0:T(8,128)(2,1)} async-done(((bf16[4096,128]{1,0:T(8,128)(2,1)}), bf16[32768,128]{1,0:T(8,128)(2,1)}) %all-gather.5.cloned.1.call-update) | async-done | bytes 8388624 | tf_op jit(solution)/shard_map/all_gather | solution.py:86
  185.9 94.8 %all-gather.3.cloned.1.call-done = bf16[32768,128]{1,0:T(8,128)(2,1)} async-done(((bf16[4096,128]{1,0:T(8,128)(2,1)}), bf16[32768,128]{1,0:T(8,128)(2,1)}) %all-gather.3.cloned.1.call-update) | async-done | bytes 8388624 | tf_op jit(solution)/shard_map/all_gather | solution.py:85
  280.6 0.2 broadcast_in_dim.45
  280.9 97.8 %while.15 = (s32[]{:T(128)}, f32[32,128]{1,0:T(8,128)S(1)}, f32[32,128]{1,0:T(8,128)S(1)}, f32[32,128,128]{2,1,0:T(8,128)S(1)}, s32[]{:T(128)}, /*index=5*/s32[3...) while((s32[]{:T(128)}, f32[32,128]{1,0:T(8,128)S(1)}, ...), condition=%wide.region_6.7_spmd.clone, body=%wide.region_3.6_spmd.clone.sunk | while | flops 2203073536 | bytes 173299376 | solution.py:57
  281.3 2.0 gather_fusion
  283.4 0.1 compare_select_fusion.3
  283.6 11.6 %gather_fusion.1 = bf16[256,128,128]{2,1,0:T(8,128)(2,1)} fusion(bf16[256,128,128]{2,1,0:T(8,128)(2,1)} %get-tuple-element.267, s32[1024]{0:T(1024)S(1)} %pad_clamp_fusion.2), kind=kCustom, calls=%fused_computation.clone.clone.1 | custom fusion | bytes 16778240 | tf_op jit(solution)/shard_map/while/body/gather | solution.py:34
  295.3 5.6 %bitcast_reduce_fusion.2 = (f32[32,128]{1,0:T(8,128)S(1)}, f32[32,8,128,128]{3,2,1,0:T(8,128)S(1)}) fusion(pred[32,8]{1,0:T(8,128)(4,1)S(1)} %broadcast_compare_fusion.2, bf16[32,8,128,128]{3,2,1,0:T(8,128)(2,1)} %bitcast.72, bf16[32,128,128]{2,1,0:T(8,128)(2,1)S(1)} %get-tuple-element.268), kind=kOutput, calls=%fused_computation.5.clone.1 | convolution fusion | flops 1086320640 | bytes 26231040 | tf_op jit(solution)/shard_map/while/body/qtd,qskd->qtsk/dot_general | solution.py:37
  300.9 6.0 %fusion.34 = f32[32,128]{1,0:T(8,128)S(1)} fusion(f32[32,8,128,128]{3,2,1,0:T(8,128)S(1)} %get-tuple-element.230, f32[32,128]{1,0:T(8,128)S(1)} %max.20, pred[32,8]{1,0:T(8,128)(4,1)S(1)} %broadcast_compare_fusion.2), kind=kLoop, calls=%fused_computation.10.clone.1 | loop fusion | flops 20967424 | bytes 16810240 | tf_op jit(solution)/shard_map/while/body/reduce_sum | solution.py:47
  306.9 11.6 %gather_fusion.2 = bf16[256,128,128]{2,1,0:T(8,128)(2,1)} fusion(bf16[256,128,128]{2,1,0:T(8,128)(2,1)} %get-tuple-element.269, s32[1024]{0:T(1024)S(1)} %pad_clamp_fusion.2), kind=kCustom, calls=%fused_computation.1.clone.clone.1 | custom fusion | bytes 16778240 | tf_op jit(solution)/shard_map/while/body/gather | solution.py:35
  318.5 11.4 %bitcast_add_fusion.2 = f32[32,128,128]{2,1,0:T(8,128)S(1)} fusion(f32[32,128,128]{2,1,0:T(8,128)S(1)} %get-tuple-element.249, bf16[32,8,128,128]{3,2,1,0:T(8,128)(2,1)} %bitcast.75, f32[32,8,128,128]{3,2,1,0:T(8,128)} %copy-done.1, f32[32,128]{1,0:T(8,128)S(1)} %max.20, pred[32,8]{1,0:T(8,128)(4,1)S(1)} %broadcast_compare_fusion.2, ...), kind=kOutput, calls=%fused_computation.18.clone.1 | convolution fusion | flops 1095761920 | bytes 29393152 | tf_op jit(solution)/shard_map/while/body/qtsk,qskd->qtd/dot_general | solution.py:48
  330.1 2.0 gather_fusion
  332.2 0.1 compare_select_fusion.3
  332.4 11.6 %gather_fusion.1 = bf16[256,128,128]{2,1,0:T(8,128)(2,1)} fusion(bf16[256,128,128]{2,1,0:T(8,128)(2,1)} %get-tuple-element.267, s32[1024]{0:T(1024)S(1)} %pad_clamp_fusion.2), kind=kCustom, calls=%fused_computation.clone.clone.1 | custom fusion | bytes 16778240 | tf_op jit(solution)/shard_map/while/body/gather | solution.py:34
  344.1 5.6 %bitcast_reduce_fusion.2 = (f32[32,128]{1,0:T(8,128)S(1)}, f32[32,8,128,128]{3,2,1,0:T(8,128)S(1)}) fusion(pred[32,8]{1,0:T(8,128)(4,1)S(1)} %broadcast_compare_fusion.2, bf16[32,8,128,128]{3,2,1,0:T(8,128)(2,1)} %bitcast.72, bf16[32,128,128]{2,1,0:T(8,128)(2,1)S(1)} %get-tuple-element.268), kind=kOutput, calls=%fused_computation.5.clone.1 | convolution fusion | flops 1086320640 | bytes 26231040 | tf_op jit(solution)/shard_map/while/body/qtd,qskd->qtsk/dot_general | solution.py:37
  349.7 6.0 %fusion.34 = f32[32,128]{1,0:T(8,128)S(1)} fusion(f32[32,8,128,128]{3,2,1,0:T(8,128)S(1)} %get-tuple-element.230, f32[32,128]{1,0:T(8,128)S(1)} %max.20, pred[32,8]{1,0:T(8,128)(4,1)S(1)} %broadcast_compare_fusion.2), kind=kLoop, calls=%fused_computation.10.clone.1 | loop fusion | flops 20967424 | bytes 16810240 | tf_op jit(solution)/shard_map/while/body/reduce_sum | solution.py:47
  355.7 11.6 %gather_fusion.2 = bf16[256,128,128]{2,1,0:T(8,128)(2,1)} fusion(bf16[256,128,128]{2,1,0:T(8,128)(2,1)} %get-tuple-element.269, s32[1024]{0:T(1024)S(1)} %pad_clamp_fusion.2), kind=kCustom, calls=%fused_computation.1.clone.clone.1 | custom fusion | bytes 16778240 | tf_op jit(solution)/shard_map/while/body/gather | solution.py:35
  367.3 11.4 %bitcast_add_fusion.2 = f32[32,128,128]{2,1,0:T(8,128)S(1)} fusion(f32[32,128,128]{2,1,0:T(8,128)S(1)} %get-tuple-element.249, bf16[32,8,128,128]{3,2,1,0:T(8,128)(2,1)} %bitcast.75, f32[32,8,128,128]{3,2,1,0:T(8,128)} %copy-done.1, f32[32,128]{1,0:T(8,128)S(1)} %max.20, pred[32,8]{1,0:T(8,128)(4,1)S(1)} %broadcast_compare_fusion.2, ...), kind=kOutput, calls=%fused_computation.18.clone.1 | convolution fusion | flops 1095761920 | bytes 29393152 | tf_op jit(solution)/shard_map/while/body/qtsk,qskd->qtd/dot_general | solution.py:48
  378.7 0.7 divide_convert_fusion
  379.4 35.0 %all_to_all.72 = bf16[32,128,128]{2,1,0:T(8,128)(2,1)S(1)} all-to-all(bf16[32,128,128]{2,1,0:T(8,128)(2,1)S(1)} %divide_convert_fusion), channel_id=1, replica_groups=mesh['blk'=8,'head'=32] {'head'}, dimensions={0} | all-to-all | bytes 2097152 | tf_op jit(solution)/shard_map/all_to_all | solution.py:107
  414.5 1.1 copy_bitcast_fusion
  (35 shorter events, 1.0 us)
Async XLA Ops:
  6.5 92.0 %copy-start.2 = (bf16[128,4096]{1,0:T(8,128)(2,1)S(1)}, bf16[128,4096]{1,0:T(8,128)(2,1)}, u32[]{:S(2)}) copy-start(bf16[128,4096]{1,0:T(8,128)(2,1)} %param.6) | copy-start | bytes 3145732
  6.5 179.3 %all-gather.5.cloned.1.call-start = ((), (), s32[]{:S(2)}) async-start(), calls=%async_computation.5 | async-start | bytes 9437184 | tf_op jit(solution)/shard_map/all_gather | solution.py:86
  8.2 96.7 %copy-start = (s32[1,32,16]{1,2,0:T(8,128)S(1)}, s32[1,32,16]{1,2,0:T(8,128)}, u32[]{:S(2)}) copy-start(s32[1,32,16]{1,2,0:T(8,128)} %param.9) | copy-start | bytes 6148
  50.5 230.1 %all-gather.3.cloned.1.call-start = ((), (), s32[]{:S(2)}) async-start(), calls=%async_computation.4 | async-start | bytes 9437184 | tf_op jit(solution)/shard_map/all_gather | solution.py:85
  99.9 46.0 %all-to-all-start.1 = ((bf16[128,32,128]{0,2,1:T(8,128)(2,1)}), bf16[128,32,128]{0,2,1:T(8,128)(2,1)S(1)}, u32[]{:S(2)}, u32[]{:S(2)}) async-start(bf16[128,32,128]{0,2,1:T(8,128)(2,1)} %bitcast.5), calls=%async_computation.1 | async-start | bytes 2097152 | tf_op jit(solution)/shard_map/all_to_all | solution.py:62
  300.9 6.0 %copy-start.1 = (f32[32,8,128,128]{3,2,1,0:T(8,128)}, f32[32,8,128,128]{3,2,1,0:T(8,128)S(1)}, u32[]{:S(2)}) copy-start(f32[32,8,128,128]{3,2,1,0:T(8,128)S(1)} %get-tuple-element.230) | copy-start | bytes 50331652 | tf_op jit(solution)/shard_map/while
  349.7 6.0 %copy-start.1 = (f32[32,8,128,128]{3,2,1,0:T(8,128)}, f32[32,8,128,128]{3,2,1,0:T(8,128)S(1)}, u32[]{:S(2)}) copy-start(f32[32,8,128,128]{3,2,1,0:T(8,128)S(1)} %get-tuple-element.230) | copy-start | bytes 50331652 | tf_op jit(solution)/shard_map/while
Sparse Core Ops, SparseCore 0:
  50.6 135.1 all-gather.4
  187.6 92.9 all-gather.2
where the time goes:
time: 427 us; the launch traced here: 422 us
  waiting for transfers between devices  174 us (41%)
  blocking collectives  122 us (29%)
  local copies, waits for them, and re-layouts  58.9 us (14%)
  matrix products  34 us (8%)
  between operations  14.1 us (3%)
  other arithmetic  13.9 us (3%)
  starting transfers between devices  5.07 us (1%)
    all_gather x1, waiting for transfers between devices, on_device(): lax.all_gather(key_local, 'blk', axis=0, tiled=True)  94.8 us
    all_to_all x1, blocking collectives, on_device(): lax.all_to_all(key_rows, 'head', split_axis=1, concat_axis=0, tiled=True)  45.7 us
    all_to_all x1, blocking collectives, on_device(): lax.all_to_all(value_rows, 'head', split_axis=1, concat_axis=0, tiled=True)  41.6 us
    all_to_all x1, waiting for transfers between devices, on_device(): lax.all_to_all(query_rows, 'head', split_axis=1, concat_axis=0, tiled=True)  39.6 us
    all_gather x1, waiting for transfers between devices, on_device(): lax.all_gather(value_local, 'blk', axis=0, tiled=True)  39.3 us
    all_to_all x1, blocking collectives, on_device(): lax.all_to_all(blended, 'head', split_axis=0, concat_axis=1, tiled=True)  35 us
    gather x2, local copies, waits for them, and re-layouts, one_turn(): picked_keys = key_blocks[relative]  23.2 us
    gather x2, local copies, waits for them, and re-layouts, one_turn(): picked_values = value_blocks[relative]  23.1 us
  transfers between devices with their start and end apart: 3, of which 3 were waited for; matrix products, arithmetic and copies ran while one was open for 1% of the time, Pallas kernels for 0%

commit v1 on v0

v1 whole, which is shorter than its diff:
```python
import math

import jax
import jax.numpy as jnp
from jax import lax
from jax.experimental import pallas as pl
from jax.experimental.pallas import tpu as pltpu
from jax.sharding import PartitionSpec as P

MESH = pl.DeviceIdType.MESH
BLOCK = 128
LIVE = 16
NX, NY, NZ = 4, 4, 8
EXP_SCALE = (128**-0.5) * math.log2(math.e)


def device(x, y, z, c):
    return ((z % 2) * NX + x, (y * (NZ // 2) + z // 2) * 2 + c)


def dz_of(g):
    return jnp.where(g % 2 == 1, (g + 1) // 2, (NZ - g // 2) % NZ)


def remote(src, dst, send_sem, recv_sem, to):
    copy = pltpu.make_async_remote_copy(
        src_ref=src, dst_ref=dst, send_sem=send_sem, recv_sem=recv_sem, device_id=to, device_id_type=MESH
    )
    copy.start()


def attend(q, ks, vs):
    s = lax.dot_general(q, jnp.concatenate(ks, axis=0), (((1,), (1,)), ((), ())), preferred_element_type=jnp.float32)
    m = jnp.max(s, axis=1, keepdims=True)
    p = jnp.exp2((s - m) * EXP_SCALE)
    total = jnp.sum(p, axis=1, keepdims=True)
    o = lax.dot_general(
        p.astype(jnp.bfloat16), jnp.concatenate(vs, axis=0), (((1,), (0,)), ((), ())), preferred_element_type=jnp.float32
    )
    return (o / total).astype(jnp.bfloat16)


def kernel(
    q_hbm, k_hbm, v_hbm, lists_hbm, out_hbm,
    kv, qbuf, obuf, lists_v, slots_v, slots,
    a_send, a_recv, x_send, left_recv, right_recv, far_recv, c_send, c_recv,
    l_send, l_recv, s_sem, o_send, o_recv,
):
    blk, head = lax.axis_index("blk"), lax.axis_index("head")
    x, z_lo = blk % NX, blk // NX
    y, z_hi, c = head // NZ, (head // 2) % (NZ // 2), head % 2
    z = z_hi * 2 + z_lo
    right, left = device((x + 1) % NX, y, z, c), device((x + NX - 1) % NX, y, z, c)
    other = device(x, y, z, 1 - c)
    my_head = y * NZ + z

    def slab(xx, zz):
        return ((c * NX + xx) * NZ + zz) * NY

    barrier = pltpu.get_barrier_semaphore()

    def greet(to):
        pl.semaphore_signal(barrier, inc=1, device_id=to, device_id_type=MESH)

    for dy in range(NY):
        for dz in range(NZ):
            if dy or dz:
                greet(device(x, (y + dy) % NY, (z + dz) % NZ, c))
    greet(right)
    greet(left)
    greet(other)
    greet(device(x, y, z + 1 - 2 * z_lo, 1 - c))
    pl.semaphore_wait(barrier, NY * NZ - 1 + 4)

    owner_z = z_hi * 2 + c
    remote(lists_hbm.at[0], lists_v.at[z_lo], l_send, l_recv, device(x, y, owner_z, 1 - c))

    @pl.when(z_lo == c)
    def _():
        pltpu.make_async_copy(lists_hbm.at[0], lists_v.at[z_lo], l_recv).start()

    @pl.when(z_lo != c)
    def _():
        remote(lists_hbm.at[0], lists_v.at[z_lo], l_send, l_recv, device(x, y, owner_z, c))

    for t, rows in enumerate((k_hbm, v_hbm, q_hbm)):

        def target(zz, yy, t=t):
            return qbuf.at[zz * NY + yy] if t == 2 else kv.at[t, slab(x, zz) + yy]

        def piece(zz, yy, rows=rows):
            return rows.at[:, pl.ds(pl.multiple_of((yy * NZ + zz) * BLOCK, BLOCK), BLOCK)]

        pltpu.make_async_copy(piece(z, y), target(z, y), a_recv.at[t, 0]).start()
        for dy in range(1, NY):
            yy = (y + dy) % NY
            remote(piece(z, yy), target(z, y), a_send.at[t], a_recv.at[t, 0], device(x, yy, z, c))

        def send(g, _, t=t, piece=piece, target=target):
            zz = (z + dz_of(g)) % NZ
            for dy in range(NY):
                yy = (y + dy) % NY
                remote(piece(zz, yy), target(z, y), a_send.at[t], a_recv.at[t, g], device(x, yy, zz, c))
            return 0

        lax.fori_loop(1, NZ, send, 0)

    steps = 2 * NZ

    def wait(ref, sem):
        pltpu.make_async_copy(ref, ref, sem).wait()

    def gather(s, _):
        @pl.when(s < steps)
        def _():
            t, g = s // NZ, s % NZ
            zz = (z + NZ - dz_of(g)) % NZ
            own = kv.at[t, pl.ds(slab(x, zz), NY)]
            wait(own, a_recv.at[t, g])
            remote(own, own, x_send.at[0], left_recv.at[t, g], right)
            remote(own, own, x_send.at[1], right_recv.at[t, g], left)
            remote(own, own, c_send, c_recv, other)

        @pl.when((s >= 2) & (s < steps + 2))
        def _():
            t, g = (s - 2) // NZ, (s - 2) % NZ
            zz = (z + NZ - dz_of(g)) % NZ
            base = slab((x + NX - 1) % NX, zz)
            chunk = kv.at[t, pl.ds(base, NY)]
            half = kv.at[t, pl.ds(base, NY // 2)]
            wait(chunk, left_recv.at[t, g])
            remote(half, half, x_send.at[2], far_recv.at[t, g], right)
            remote(chunk, chunk, c_send, c_recv, other)
            base = slab((x + 1) % NX, zz)
            chunk = kv.at[t, pl.ds(base, NY)]
            half = kv.at[t, pl.ds(base + NY // 2, NY // 2)]
            wait(chunk, right_recv.at[t, g])
            remote(half, half, x_send.at[2], far_recv.at[t, g], left)
            remote(chunk, chunk, c_send, c_recv, other)

        @pl.when(s >= 4)
        def _():
            t, g = (s - 4) // NZ, (s - 4) % NZ
            zz = (z + NZ - dz_of(g)) % NZ
            chunk = kv.at[t, pl.ds(slab((x + 2) % NX, zz), NY)]
            wait(chunk, far_recv.at[t, g])
            remote(chunk, chunk, c_send, c_recv, other)

        return 0

    lax.fori_loop(0, steps + 4, gather, 0)

    wait(lists_v, l_recv)
    i = lists_v[...]
    slots_v[...] = (((i & 1) * NX + ((i >> 5) & 3)) * NZ + ((i >> 1) & 3) * 2 + (i >> 7)) * NY + ((i >> 3) & 3)
    to_smem = pltpu.make_async_copy(slots_v, slots, s_sem)
    to_smem.start()
    to_smem.wait()

    for g in range(NZ):
        zz = (z + NZ - dz_of(g)) % NZ
        wait(qbuf.at[pl.ds(zz * NY, NY)], a_recv.at[2, g])
    wait(kv.at[:, pl.ds((1 - c) * NX * NZ * NY, NX * NZ * NY)], c_recv)

    def one_block(dy, dz):
        yy, zz = (y + dy) % NY, (z + dz) % NZ
        row = (yy * (NZ // 2) + zz // 2) * 2 + c
        places = [slots[zz % 2, row, j] for j in range(LIVE)]
        n = zz * NY + yy
        obuf[n] = attend(qbuf[n], [kv[0, p] for p in places], [kv[1, p] for p in places])
        mine = out_hbm.at[:, pl.ds(pl.multiple_of(my_head * BLOCK, BLOCK), BLOCK)]
        return obuf.at[n], mine, device(x, yy, zz, c)

    def pair(p, _):
        near, r = p - 14, p - 2
        dz_a = jnp.where(p < 2, 4, jnp.where(p < 14, 3 - r // 4, 0))
        dz_b = (NZ - dz_a) % NZ
        dy_a = jnp.where(p < 2, 2 * p, jnp.where(p < 14, (r + NY) % NY, 1 + near))
        dy_b = jnp.where(p < 2, 2 * p + 1, jnp.where(p < 14, (r + NY) % NY, (3 - 3 * near + NY) % NY))
        src_a, mine, to_a = one_block(dy_a, dz_a)
        remote(src_a, mine, o_send, o_recv, to_a)
        src_b, mine, to_b = one_block(dy_b, dz_b)

        @pl.when(p < 15)
        def _():
            remote(src_b, mine, o_send, o_recv, to_b)

        @pl.when(p == 15)
        def _():
            pltpu.make_async_copy(src_b, mine, o_recv).start()

        return 0

    lax.fori_loop(0, 16, pair, 0)

    for t in range(3):
        wait(kv.at[0, pl.ds(0, NY * NZ - 1)], a_send.at[t])
    for i in range(3):
        wait(kv.at[:, pl.ds(0, NZ * NY)], x_send.at[i])
    wait(kv.at[:, pl.ds(c * NX * NZ * NY, NX * NZ * NY)], c_send)
    wait(lists_v.at[0], l_send)

    @pl.when(z_lo != c)
    def _():
        wait(lists_v.at[0], l_send)

    wait(obuf.at[pl.ds(0, NY * NZ - 1)], o_send)
    wait(out_hbm, o_recv)


def on_device(query_rows, key_rows, value_rows, block_lists):
    dma = pltpu.SemaphoreType.DMA
    return pl.pallas_call(
        kernel,
        out_shape=jax.ShapeDtypeStruct(query_rows.shape, jnp.bfloat16),
        in_specs=[pl.BlockSpec(memory_space=pl.ANY)] * 4,
        out_specs=pl.BlockSpec(memory_space=pl.ANY),
        scratch_shapes=[
            pltpu.VMEM((2, 256, BLOCK, BLOCK), jnp.bfloat16),
            pltpu.VMEM((NY * NZ, BLOCK, BLOCK), jnp.bfloat16),
            pltpu.VMEM((NY * NZ, BLOCK, BLOCK), jnp.bfloat16),
            pltpu.VMEM((2, 32, LIVE), jnp.int32),
            pltpu.VMEM((2, 32, LIVE), jnp.int32),
            pltpu.SMEM((2, 32, LIVE), jnp.int32),
            dma((3,)), dma((3, NZ)), dma((3,)), dma((2, NZ)), dma((2, NZ)), dma((2, NZ)), dma, dma,
            dma, dma, dma, dma, dma,
        ],
        compiler_params=pltpu.CompilerParams(collective_id=0, has_side_effects=True, vmem_limit_bytes=48 * 2**20),
        name="attention",
    )(query_rows, key_rows, value_rows, block_lists)


def solution(mesh):
    in_specs = (P(("blk", "head"), None), P(("blk", "head"), None), P(("blk", "head"), None), P("head", "blk", None))
    return jax.shard_map(
        on_device, mesh=mesh, in_specs=in_specs, out_specs=P(("blk", "head"), None), check_vma=False
    )
```

time: 427 us -> 123 us (0.29)
  waiting for transfers between devices: 174 us -> 0 us
  blocking collectives: 122 us -> 0 us
  Pallas kernels: 0 us -> 117 us
  local copies, waits for them, and re-layouts: 58.9 us -> 5.42 us
  matrix products: 34 us -> 0 us
  between operations: 14.1 us -> 0.01 us
  other arithmetic: 13.9 us -> 0 us
  starting transfers between devices: 5.07 us -> 0 us
    all_gather x2 -> x0, waiting for transfers between devices: 134 us -> none  [the longest x1 94.8 us: on_device(): lax.all_gather(key_local, 'blk', axis=0, tiled=True)]
    all_to_all x3 -> x0, blocking collectives: 122 us -> none  [the longest x1 45.7 us: on_device(): lax.all_to_all(key_rows, 'head', split_axis=1, concat_axis=0, tiled=True)]
    pallas_call x0 -> x1, Pallas kernels: none -> 117 us  [on_device(): pl.pallas_call(kernel, out_shape=jax.ShapeDtypeStruct(query_rows.shape, j...]
    gather x10 -> x0, local copies, waits for them, and re-layouts: 50.7 us -> none  [the longest x2 23.2 us: one_turn(): picked_keys = key_blocks[relative]]
    all_to_all x1 -> x0, waiting for transfers between devices: 39.6 us -> none  [on_device(): lax.all_to_all(query_rows, 'head', split_axis=1, concat_axis=0, tiled=True)]
    dot_general x4 -> x0, matrix products: 34 us -> none  [the longest x2 22.8 us: one_turn(): jnp.einsum('qtsk,qskd->qtd', weights.astype(jnp.bfloat16), picked_values,...]
    reduce_sum x3 -> x0, other arithmetic: 12 us -> none  [the longest x2 12 us: one_turn(): running_sum = running_sum * factor + jnp.sum(weights, axis=(2, 3))]
    all_to_all x1 -> x0, starting transfers between devices: 5.02 us -> none  [on_device(): lax.all_to_all(query_rows, 'head', split_axis=1, concat_axis=0, tiled=True)]
  transfers between devices with their start and end apart: 3 -> 0, of which waited for: 3 -> 0; matrix products, arithmetic and copies ran while one was open for 1% -> 0% of each run, Pallas kernels for 0% -> 0%
where the time goes in v1:
time: 123 us
  Pallas kernels  117 us (95%)
  local copies, waits for them, and re-layouts  5.42 us (4%)
    pallas_call x1, Pallas kernels, on_device(): pl.pallas_call(kernel, out_shape=jax.ShapeDtypeStruct(query_rows.shape, j...  117 us
    unnamed x8, local copies, waits for them, and re-layouts  5.42 us

profile of v1, /device:TPU:1, one launch (start us, length us, event | category | flops | bytes accessed | tf_op | source)
XLA Modules:
  0.0 122.5 jit_solution(18431280409997729942)
XLA Ops:
  0.0 0.8 copy.5.lists_hbm
  0.8 0.0 copy-start
  0.8 1.2 copy-done
  2.0 0.0 copy-start.1
  2.0 1.2 copy-done.1
  3.2 0.0 copy-start.2
  3.2 1.2 copy-done.2
  4.4 117.1 %attention.1 = bf16[128,4096]{1,0:T(8,128)(2,1)S(1)} custom-call(bf16[128,4096]{1,0:T(8,128)(2,1)S(1)} %copy-done, bf16[128,4096]{1,0:T(8,128)(2,1)S(1)} %copy-done.1, bf16[128,4096]{1,0:T(8,128)(2,1)S(1)} %copy-done.2, s32[1,32,16]{2,1,0:T(8,128)S(1)} %copy.5.lists_hbm), custom_call_target="tpu_custom_call" | custom-call | tf_op jit(solution)/shard_map/attention/pallas_call | solution.py:213
  121.6 1.0 copy.7
Async XLA Ops:
  0.8 1.2 %copy-start = (bf16[128,4096]{1,0:T(8,128)(2,1)S(1)}, bf16[128,4096]{1,0:T(8,128)(2,1)}, u32[]{:S(2)}) copy-start(bf16[128,4096]{1,0:T(8,128)(2,1)} %q_hbm.1) | copy-start | bytes 3145732
  2.0 1.2 copy-start.1
  3.2 1.2 copy-start.2

commit v2 on v1

v2 whole, which is shorter than its diff:
```python
import math

import jax
import jax.numpy as jnp
from jax import lax
from jax.experimental import pallas as pl
from jax.experimental.pallas import tpu as pltpu
from jax.sharding import PartitionSpec as P

MESH = pl.DeviceIdType.MESH
BLOCK = 128
LIVE = 16
NX, NY, NZ = 4, 4, 8
HALF = NX * NY * NZ
EXP_SCALE = (128**-0.5) * math.log2(math.e)


def device(x, y, z, c):
    return ((z % 2) * NX + x, (y * (NZ // 2) + z // 2) * 2 + c)


def dz_of(g):
    return jnp.where(g % 2 == 1, (g + 1) // 2, (NZ - g // 2) % NZ)


def remote(src, dst, send_sem, recv_sem, to):
    copy = pltpu.make_async_remote_copy(
        src_ref=src, dst_ref=dst, send_sem=send_sem, recv_sem=recv_sem, device_id=to, device_id_type=MESH
    )
    copy.start()


def wait(ref, sem):
    pltpu.make_async_copy(ref, ref, sem).wait()


def kernel(
    q_hbm, k_hbm, v_hbm, lists_hbm, out_hbm,
    kbuf, vbuf, qbuf, obuf, weights, totals, lists_v, slots_v, slots,
    a_send, near_recv, a_recv, x_send, left_recv, right_recv, far_recv, c_send, c_recv,
    l_send, l_recv, s_sem, o_send, o_recv,
):
    blk, head = lax.axis_index("blk"), lax.axis_index("head")
    x, z_lo = blk % NX, blk // NX
    y, z_hi, c = head // NZ, (head // 2) % (NZ // 2), head % 2
    z = z_hi * 2 + z_lo
    right, left = device((x + 1) % NX, y, z, c), device((x + NX - 1) % NX, y, z, c)
    other = device(x, y, z, 1 - c)
    my_head = y * NZ + z

    kv = (kbuf, vbuf)

    def slab(xx, zz):
        return ((c * NX + xx) * NZ + zz) * NY

    barrier = pltpu.get_barrier_semaphore()

    def greet(to):
        pl.semaphore_signal(barrier, inc=1, device_id=to, device_id_type=MESH)

    for dy in range(NY):
        for dz in range(NZ):
            if dy or dz:
                greet(device(x, (y + dy) % NY, (z + dz) % NZ, c))
    greet(right)
    greet(left)
    greet(other)
    greet(device(x, y, z + 1 - 2 * z_lo, 1 - c))
    pl.semaphore_wait(barrier, NY * NZ - 1 + 4)

    def target(t, zz, yy):
        return qbuf.at[zz * NY + yy] if t == 2 else kv[t].at[slab(x, zz) + yy]

    def piece(t, zz, yy):
        rows = (k_hbm, v_hbm, q_hbm)[t]
        return rows.at[:, pl.ds(pl.multiple_of((yy * NZ + zz) * BLOCK, BLOCK), BLOCK)]

    def send_near(t):
        for dy in (1, 3, 2):
            yy = (y + dy) % NY
            sem = a_recv.at[t, 0] if t == 2 else near_recv.at[t, dy]
            remote(piece(t, z, yy), target(t, z, y), a_send.at[t], sem, device(x, yy, z, c))
        sem = a_recv.at[t, 0] if t == 2 else near_recv.at[t, 0]
        pltpu.make_async_copy(piece(t, z, y), target(t, z, y), sem).start()

    def send(t, g, ways):
        zz = (z + dz_of(g)) % NZ
        for dy in ways:
            yy = (y + dy) % NY
            remote(piece(t, zz, yy), target(t, z, y), a_send.at[t], a_recv.at[t, g], device(x, yy, zz, c))

    def send_all(t, first, ways):
        lax.fori_loop(first, NZ, lambda g, _: (send(t, g, ways), 0)[1], 0)

    def from_z(g):
        return (z + NZ - dz_of(g)) % NZ

    def to_both(src, dst, t, g):
        remote(src, dst, x_send.at[0], left_recv.at[t, g], right)
        remote(src, dst, x_send.at[1], right_recv.at[t, g], left)

    def gather_own_block(t):
        to_both(piece(t, z, y), kv[t].at[slab(x, z) + y], t, 0)

    def gather_near_block(t, dy):
        block = kv[t].at[slab(x, z) + (y + NY - dy) % NY]
        wait(block, near_recv.at[t, dy])
        to_both(block, block, t, 0)

    def swap_own_plane(t):
        wait(kv[t].at[slab(x, z) + y], near_recv.at[t, 0])
        own = kv[t].at[pl.ds(slab(x, z), NY)]
        remote(own, own, c_send, c_recv.at[t], other)

    def take_own(t, g):
        own = kv[t].at[pl.ds(slab(x, from_z(g)), NY)]
        wait(own, a_recv.at[t, g])
        to_both(own, own, t, g)
        remote(own, own, c_send, c_recv.at[t], other)

    def take_sides(t, g):
        base = slab((x + NX - 1) % NX, from_z(g))
        chunk = kv[t].at[pl.ds(base, NY)]
        half = kv[t].at[pl.ds(base, NY // 2)]
        wait(chunk, left_recv.at[t, g])
        remote(half, half, x_send.at[2], far_recv.at[t, g], right)
        remote(chunk, chunk, c_send, c_recv.at[t], other)
        base = slab((x + 1) % NX, from_z(g))
        chunk = kv[t].at[pl.ds(base, NY)]
        half = kv[t].at[pl.ds(base + NY // 2, NY // 2)]
        wait(chunk, right_recv.at[t, g])
        remote(half, half, x_send.at[2], far_recv.at[t, g], left)
        remote(chunk, chunk, c_send, c_recv.at[t], other)

    def take_far(t, g):
        chunk = kv[t].at[pl.ds(slab((x + 2) % NX, from_z(g)), NY)]
        wait(chunk, far_recv.at[t, g])
        remote(chunk, chunk, c_send, c_recv.at[t], other)

    def places_of(zz, yy):
        row = (yy * (NZ // 2) + zz // 2) * 2 + c
        return [slots[zz % 2, j, row] for j in range(LIVE)]

    def score(zz, yy):
        n = zz * NY + yy
        keys = jnp.concatenate([kbuf[p] for p in places_of(zz, yy)], axis=0)
        s = lax.dot_general(qbuf[n], keys, (((1,), (1,)), ((), ())), preferred_element_type=jnp.float32)
        m = jnp.max(s, axis=1, keepdims=True)
        p = jnp.exp2((s - m) * EXP_SCALE)
        weights[n] = p.astype(jnp.bfloat16)
        totals[n] = jnp.broadcast_to(jnp.sum(p, axis=1, keepdims=True), (BLOCK, BLOCK))

    def mix(zz, yy):
        n = zz * NY + yy
        values = jnp.concatenate([vbuf[p] for p in places_of(zz, yy)], axis=0)
        o = lax.dot_general(weights[n], values, (((1,), (0,)), ((), ())), preferred_element_type=jnp.float32)
        obuf[n] = (o / totals[n]).astype(jnp.bfloat16)
        return obuf.at[n]

    gather_own_block(0)
    send_near(0)
    gather_own_block(1)
    send_near(1)
    for g in range(1, 5):
        send(0, g, (0,))

    owner_z = z_hi * 2 + c
    remote(lists_hbm.at[0], lists_v.at[z_lo], l_send, l_recv, device(x, y, owner_z, 1 - c))

    @pl.when(z_lo == c)
    def _():
        pltpu.make_async_copy(lists_hbm.at[0], lists_v.at[z_lo], l_recv).start()

    @pl.when(z_lo != c)
    def _():
        remote(lists_hbm.at[0], lists_v.at[z_lo], l_send, l_recv, device(x, y, owner_z, c))

    gather_near_block(0, 1)
    gather_near_block(0, 3)
    send(0, 1, (1, 3, 2))
    send(0, 2, (1, 3, 2))
    gather_near_block(0, 2)
    swap_own_plane(0)
    gather_near_block(1, 1)
    gather_near_block(1, 3)
    send(0, 3, (1, 3, 2))
    send(0, 4, (1, 3, 2))
    gather_near_block(1, 2)
    swap_own_plane(1)
    send(0, 5, (0, 1, 3, 2))
    send(0, 6, (0, 1, 3, 2))
    take_own(0, 1)
    take_sides(0, 0)
    send(0, 7, (0, 1, 3, 2))
    send_all(1, 1, (0, 1, 3, 2))
    take_own(0, 2)
    take_sides(1, 0)
    send_near(2)
    send_all(2, 1, (0, 1, 3, 2))
    take_own(0, 3)
    take_sides(0, 1)
    take_far(0, 0)
    take_own(0, 4)
    take_sides(0, 2)
    take_far(1, 0)

    def keys(g, _):
        take_own(0, g + 4)
        take_sides(0, g + 2)
        take_far(0, g)
        return 0

    lax.fori_loop(1, 4, keys, 0)

    def both(g, _):
        take_own(1, g)
        take_sides(0, g + 5)
        take_far(0, g + 3)
        return 0

    lax.fori_loop(1, 3, both, 0)

    def values(g, _):
        take_own(1, g + 2)
        take_sides(1, g)
        take_far(0, g + 5)
        return 0

    lax.fori_loop(1, 3, values, 0)

    wait(lists_v, l_recv)
    i = lists_v[...]
    slots_v[...] = (((i & 1) * NX + ((i >> 5) & 3)) * NZ + ((i >> 1) & 3) * 2 + (i >> 7)) * NY + ((i >> 3) & 3)
    to_smem = pltpu.make_async_copy(slots_v, slots, s_sem)
    to_smem.start()
    to_smem.wait()

    wait(kbuf.at[pl.ds((1 - c) * HALF, HALF)], c_recv.at[0])

    def score_and_gather(g, _):
        @pl.when(g < 3)
        def _():
            take_own(1, g + 5)

        @pl.when(g < 5)
        def _():
            take_sides(1, g + 3)

        @pl.when(g < 7)
        def _():
            take_far(1, g + 1)

        zz = from_z(g)
        wait(qbuf.at[pl.ds(zz * NY, NY)], a_recv.at[2, g])
        for yy in range(NY):
            score(zz, yy)
        return 0

    lax.fori_loop(0, NZ, score_and_gather, 0)
    wait(vbuf.at[pl.ds((1 - c) * HALF, HALF)], c_recv.at[1])

    mine = out_hbm.at[:, pl.ds(pl.multiple_of(my_head * BLOCK, BLOCK), BLOCK)]

    def pair(p, _):
        near, r = p - 14, p - 2
        dz_a = jnp.where(p < 2, 4, jnp.where(p < 14, 3 - r // 4, 0))
        dz_b = (NZ - dz_a) % NZ
        dy_a = jnp.where(p < 2, 2 * p, jnp.where(p < 14, (r + NY) % NY, 1 + near))
        dy_b = jnp.where(p < 2, 2 * p + 1, jnp.where(p < 14, (r + NY) % NY, (3 - 3 * near + NY) % NY))
        yy_a, zz_a, yy_b, zz_b = (y + dy_a) % NY, (z + dz_a) % NZ, (y + dy_b) % NY, (z + dz_b) % NZ
        src_a = mix(zz_a, yy_a)
        src_b = mix(zz_b, yy_b)
        remote(src_a, mine, o_send, o_recv, device(x, yy_a, zz_a, c))

        @pl.when(p < 15)
        def _():
            remote(src_b, mine, o_send, o_recv, device(x, yy_b, zz_b, c))

        @pl.when(p == 15)
        def _():
            pltpu.make_async_copy(src_b, mine, o_recv).start()

        return 0

    lax.fori_loop(0, 16, pair, 0)

    for t in range(3):
        wait(kbuf.at[pl.ds(0, NY * NZ - 1)], a_send.at[t])
    for i in range(3):
        wait(kbuf.at[pl.ds(0, 2 * NZ * NY)], x_send.at[i])
    wait(kbuf, c_send)
    wait(lists_v.at[0], l_send)

    @pl.when(z_lo != c)
    def _():
        wait(lists_v.at[0], l_send)

    wait(obuf.at[pl.ds(0, NY * NZ - 1)], o_send)
    wait(out_hbm, o_recv)


def on_device(query_rows, key_rows, value_rows, block_lists):
    dma = pltpu.SemaphoreType.DMA
    return pl.pallas_call(
        kernel,
        out_shape=jax.ShapeDtypeStruct(query_rows.shape, jnp.bfloat16),
        in_specs=[pl.BlockSpec(memory_space=pl.ANY)] * 4,
        out_specs=pl.BlockSpec(memory_space=pl.ANY),
        scratch_shapes=[
            pltpu.VMEM((2 * HALF, BLOCK, BLOCK), jnp.bfloat16),
            pltpu.VMEM((2 * HALF, BLOCK, BLOCK), jnp.bfloat16),
            pltpu.VMEM((NY * NZ, BLOCK, BLOCK), jnp.bfloat16),
            pltpu.VMEM((NY * NZ, BLOCK, BLOCK), jnp.bfloat16),
            pltpu.VMEM((NY * NZ, BLOCK, LIVE * BLOCK), jnp.bfloat16),
            pltpu.VMEM((NY * NZ, BLOCK, BLOCK), jnp.float32),
            pltpu.VMEM((2, LIVE, 32), jnp.int32),
            pltpu.VMEM((2, LIVE, 32), jnp.int32),
            pltpu.SMEM((2, LIVE, 32), jnp.int32),
            dma((3,)), dma((2, NY)), dma((3, NZ)), dma((3,)), dma((2, NZ)), dma((2, NZ)), dma((2, NZ)), dma, dma((2,)),
            dma, dma, dma, dma, dma,
        ],
        compiler_params=pltpu.CompilerParams(collective_id=0, has_side_effects=True, vmem_limit_bytes=52 * 2**20),
        name="attention",
    )(query_rows, key_rows, value_rows, jnp.swapaxes(block_lists, 1, 2))


def solution(mesh):
    in_specs = (P(("blk", "head"), None), P(("blk", "head"), None), P(("blk", "head"), None), P("head", "blk", None))
    return jax.shard_map(
        on_device, mesh=mesh, in_specs=in_specs, out_specs=P(("blk", "head"), None), check_vma=False
    )
```

time: 123 us -> 113 us (0.919)
  Pallas kernels: 117 us -> 111 us
  local copies, waits for them, and re-layouts: 5.42 us -> 1.67 us
    pallas_call x1, Pallas kernels: 117 us -> 111 us  [on_device(): pl.pallas_call(kernel, out_shape=jax.ShapeDtypeStruct(query_rows.shape, j...]
    unnamed x8 -> x3, local copies, waits for them, and re-layouts: 5.42 us -> 1.67 us
where the time goes in v2:
time: 113 us
  Pallas kernels  111 us (98%)
  local copies, waits for them, and re-layouts  1.67 us (1%)
    pallas_call x1, Pallas kernels, on_device(): pl.pallas_call(kernel, out_shape=jax.ShapeDtypeStruct(query_rows.shape, j...  111 us

profile of v2, /device:TPU:1, one launch (start us, length us, event | category | flops | bytes accessed | tf_op | source)
XLA Modules:
  0.0 113.2 jit_solution(18364108008178642117)
XLA Ops:
  0.0 0.0 copy-start
  0.0 0.7 copy-done
  0.7 111.5 %attention.1 = bf16[128,4096]{1,0:T(8,128)(2,1)S(1)} custom-call(bf16[128,4096]{1,0:T(8,128)(2,1)} %q_hbm.1, bf16[128,4096]{1,0:T(8,128)(2,1)} %k_hbm.1, bf16[128,4096]{1,0:T(8,128)(2,1)} %v_hbm.1, s32[1,16,32]{2,1,0:T(8,128)S(1)} %bitcast.1), custom_call_target="tpu_custom_call" | custom-call | tf_op jit(solution)/shard_map/attention/pallas_call | solution.py:304
  112.2 1.0 copy.6
Async XLA Ops:
  0.0 0.7 copy-start

commit v3 on v2

v3 whole, which is shorter than its diff:
```python
import math

import jax
import jax.numpy as jnp
from jax import lax
from jax.experimental import pallas as pl
from jax.experimental.pallas import tpu as pltpu
from jax.sharding import PartitionSpec as P

MESH = pl.DeviceIdType.MESH
BLOCK = 128
LIVE = 16
NX, NY, NZ = 4, 4, 8
SLABS = NX * NY * NZ
HALF = BLOCK // 2
EXP_SCALE = (128**-0.5) * math.log2(math.e)


def device(x, y, z, c):
    return ((z % 2) * NX + x, (y * (NZ // 2) + z // 2) * 2 + c)


def dz_of(g):
    return jnp.where(g % 2 == 1, (g + 1) // 2, (NZ - g // 2) % NZ)


def far_first(i):
    return jnp.clip(jnp.where(i % 2 == 1, NZ - 2 - i, NZ - i), 0, NZ - 1)


def remote(src, dst, send_sem, recv_sem, to):
    copy = pltpu.make_async_remote_copy(
        src_ref=src, dst_ref=dst, send_sem=send_sem, recv_sem=recv_sem, device_id=to, device_id_type=MESH
    )
    copy.start()


def wait(ref, sem):
    pltpu.make_async_copy(ref, ref, sem).wait()


def kernel(
    q_hbm, k_hbm, v_hbm, lists_hbm, out_hbm,
    kbuf, lobuf, hibuf, qbuf, vraw, lo_out, hi_out, weights, totals, mixed, landed, obuf, lists_v, slots_v, slots,
    v_sem, a_send, near_recv, a_recv, x_send, left_recv, right_recv, far_recv, c_send, c_recv,
    l_send, l_recv, s_sem, o_send, o_recv, f_sem,
):
    blk, head = lax.axis_index("blk"), lax.axis_index("head")
    x, z_lo = blk % NX, blk // NX
    y, z_hi, c = head // NZ, (head // 2) % (NZ // 2), head % 2
    z = z_hi * 2 + z_lo
    right, left = device((x + 1) % NX, y, z, c), device((x + NX - 1) % NX, y, z, c)
    other = device(x, y, z, 1 - c)

    kv = (kbuf, lobuf, hibuf)
    low_lanes = lax.broadcasted_iota(jnp.int32, (HALF, BLOCK), 1) < HALF

    def slab(xx, zz):
        return ((c * NX + xx) * NZ + zz) * NY

    load_v = pltpu.make_async_copy(v_hbm, vraw, v_sem)
    load_v.start()

    barrier = pltpu.get_barrier_semaphore()

    def greet(to):
        pl.semaphore_signal(barrier, inc=1, device_id=to, device_id_type=MESH)

    for dy in range(NY):
        for dz in range(NZ):
            if dy or dz:
                greet(device(x, (y + dy) % NY, (z + dz) % NZ, c))
    greet(right)
    greet(left)
    greet(other)
    greet(device(x, y, z + 1 - 2 * z_lo, 1 - c))
    def pack(h, _):
        columns = pl.ds(pl.multiple_of(h * BLOCK, BLOCK), BLOCK)
        top = vraw[0:HALF, columns].astype(jnp.float32)
        bottom = vraw[HALF:BLOCK, columns].astype(jnp.float32)
        lo_out[h] = jnp.where(low_lanes, top, pltpu.roll(bottom, HALF, 1)).astype(jnp.bfloat16)
        hi_out[h] = jnp.where(low_lanes, pltpu.roll(top, HALF, 1), bottom).astype(jnp.bfloat16)
        return 0

    load_v.wait()
    lax.fori_loop(0, NY * NZ // 2, lambda i, _: pack(2 * i + 1, pack(2 * i, 0)), 0)
    pl.semaphore_wait(barrier, NY * NZ - 1 + 4)

    def target(t, zz, yy):
        return qbuf.at[zz * NY + yy] if t == 3 else kv[t].at[slab(x, zz) + yy]

    def piece(t, zz, yy):
        if t in (1, 2):
            return (lo_out, hi_out)[t - 1].at[yy * NZ + zz]
        rows = q_hbm if t == 3 else k_hbm
        return rows.at[:, pl.ds(pl.multiple_of((yy * NZ + zz) * BLOCK, BLOCK), BLOCK)]

    def send_near(t):
        for dy in (1, 3, 2):
            yy = (y + dy) % NY
            sem = a_recv.at[t, 0] if t else near_recv.at[dy]
            remote(piece(t, z, yy), target(t, z, y), a_send.at[t], sem, device(x, yy, z, c))
        sem = a_recv.at[t, 0] if t else near_recv.at[0]
        pltpu.make_async_copy(piece(t, z, y), target(t, z, y), sem).start()

    def send(t, g, ways):
        zz = (z + dz_of(g)) % NZ
        for dy in ways:
            yy = (y + dy) % NY
            remote(piece(t, zz, yy), target(t, z, y), a_send.at[t], a_recv.at[t, g], device(x, yy, zz, c))

    def send_all(t, first, ways):
        lax.fori_loop(first, NZ, lambda g, _: (send(t, g, ways), 0)[1], 0)

    def from_z(g):
        return (z + NZ - dz_of(g)) % NZ

    def to_both(src, dst, t, g):
        remote(src, dst, x_send.at[0], left_recv.at[t, g], right)
        remote(src, dst, x_send.at[1], right_recv.at[t, g], left)

    def gather_near_block(dy):
        block = kbuf.at[slab(x, z) + (y + NY - dy) % NY]
        wait(block, near_recv.at[dy])
        to_both(block, block, 0, 0)

    def swap_own_plane():
        wait(kbuf.at[slab(x, z) + y], near_recv.at[0])
        own = kbuf.at[pl.ds(slab(x, z), NY)]
        remote(own, own, c_send, c_recv.at[0], other)

    def take_own(t, g):
        own = kv[t].at[pl.ds(slab(x, from_z(g)), NY)]
        wait(own, a_recv.at[t, g])
        to_both(own, own, t, g)
        remote(own, own, c_send, c_recv.at[t], other)

    def take_sides(t, g):
        base = slab((x + NX - 1) % NX, from_z(g))
        chunk = kv[t].at[pl.ds(base, NY)]
        half = kv[t].at[pl.ds(base, NY // 2)]
        wait(chunk, left_recv.at[t, g])
        remote(half, half, x_send.at[2], far_recv.at[t, g], right)
        remote(chunk, chunk, c_send, c_recv.at[t], other)
        base = slab((x + 1) % NX, from_z(g))
        chunk = kv[t].at[pl.ds(base, NY)]
        half = kv[t].at[pl.ds(base + NY // 2, NY // 2)]
        wait(chunk, right_recv.at[t, g])
        remote(half, half, x_send.at[2], far_recv.at[t, g], left)
        remote(chunk, chunk, c_send, c_recv.at[t], other)

    def take_far(t, g):
        chunk = kv[t].at[pl.ds(slab((x + 2) % NX, from_z(g)), NY)]
        wait(chunk, far_recv.at[t, g])
        remote(chunk, chunk, c_send, c_recv.at[t], other)

    def from_other_core(t):
        wait(kv[t].at[pl.ds((1 - c) * SLABS, SLABS)], c_recv.at[t])

    def places_of(zz, yy):
        row = (yy * (NZ // 2) + zz // 2) * 2 + c
        return [slots[zz % 2, j, row] for j in range(LIVE)]

    def score(zz, yy):
        n = zz * NY + yy
        places = places_of(zz, yy)
        keys = [kbuf[p, 0:HALF] for p in places] + [kbuf[p, HALF:BLOCK] for p in places]
        s = lax.dot_general(
            qbuf[n], jnp.concatenate(keys, axis=0), (((1,), (1,)), ((), ())), preferred_element_type=jnp.float32
        )
        m = jnp.max(s, axis=1, keepdims=True)
        p = jnp.exp2((s - m) * EXP_SCALE)
        weights[n, 0:BLOCK] = p[:, : LIVE * HALF].astype(jnp.bfloat16)
        weights[n, BLOCK : 2 * BLOCK] = p[:, LIVE * HALF :].astype(jnp.bfloat16)
        total = jnp.broadcast_to(jnp.sum(p, axis=1, keepdims=True), (BLOCK, BLOCK))
        totals[n] = jnp.where(low_lanes, total[0:HALF], total[HALF:BLOCK])

    def mix(half, zz, yy):
        n = zz * NY + yy
        values = jnp.concatenate([kv[1 + half][p] for p in places_of(zz, yy)], axis=0)
        o = lax.dot_general(weights[n], values, (((1,), (0,)), ((), ())), preferred_element_type=jnp.float32)
        straight = jnp.where(low_lanes, o[0:HALF], o[3 * HALF : 4 * HALF])
        crossed = jnp.where(low_lanes, o[HALF : 2 * HALF], o[2 * HALF : 3 * HALF])
        mixed[half, n] = ((straight + pltpu.roll(crossed, HALF, 1)) / totals[n]).astype(jnp.bfloat16)
        return mixed.at[half, n]

    def mix_group(half, g):
        zz = from_z(g)
        ways = (1, 3, 2, 0)
        made = [mix(half, zz, (y + dy) % NY) for dy in ways]
        place = landed.at[half, z * NY + y]
        for dy, src in zip(ways, made):
            to = device(x, (y + dy) % NY, zz, c)
            if dy:
                remote(src, place, o_send.at[half], o_recv.at[half, g], to)
                continue

            @pl.when(g > 0)
            def _(src=src, to=to):
                remote(src, place, o_send.at[half], o_recv.at[half, g], to)

            @pl.when(g == 0)
            def _(src=src):
                pltpu.make_async_copy(src, place, o_recv.at[half, g]).start()

    to_both(piece(0, z, y), kbuf.at[slab(x, z) + y], 0, 0)
    for t in range(3):
        send_near(t)
    send_all(0, 1, (0,))

    owner_z = z_hi * 2 + c
    remote(lists_hbm.at[0], lists_v.at[z_lo], l_send, l_recv, device(x, y, owner_z, 1 - c))

    @pl.when(z_lo == c)
    def _():
        pltpu.make_async_copy(lists_hbm.at[0], lists_v.at[z_lo], l_recv).start()

    @pl.when(z_lo != c)
    def _():
        remote(lists_hbm.at[0], lists_v.at[z_lo], l_send, l_recv, device(x, y, owner_z, c))

    def step(count, *takes):
        def body(g, _):
            for take, t, ahead in takes:
                take(t, g + ahead)
            return 0

        lax.fori_loop(0, count, body, 0)

    gather_near_block(1)
    gather_near_block(3)
    send(0, 1, (1, 3, 2))
    send(0, 2, (1, 3, 2))
    gather_near_block(2)
    swap_own_plane()
    take_own(1, 0)
    send(0, 3, (1, 3, 2))
    send(0, 4, (1, 3, 2))
    take_own(2, 0)
    send(0, 5, (1, 3, 2))
    send(0, 6, (1, 3, 2))
    take_own(0, 1)
    take_sides(0, 0)
    send(0, 7, (1, 3, 2))
    send_all(1, 1, (0, 1, 3, 2))
    take_own(0, 2)
    take_sides(1, 0)
    send_near(3)
    lax.fori_loop(1, 5, lambda g, _: (send(3, g, (0, 1, 3, 2)), 0)[1], 0)
    take_own(0, 3)
    take_sides(2, 0)
    take_far(0, 0)
    send_all(2, 1, (0, 1, 3, 2))
    send_all(3, 5, (0, 1, 3, 2))
    take_own(0, 4)
    take_sides(0, 1)
    take_far(1, 0)
    take_sides(0, 2)
    take_far(2, 0)
    step(3, (take_own, 0, 5), (take_sides, 0, 3), (take_far, 0, 1))
    step(2, (take_own, 1, 1), (take_sides, 0, 6), (take_far, 0, 4))
    step(2, (take_own, 1, 3), (take_sides, 1, 1), (take_far, 0, 6))

    wait(lists_v, l_recv)
    i = lists_v[...]
    slots_v[...] = (((i & 1) * NX + ((i >> 5) & 3)) * NZ + ((i >> 1) & 3) * 2 + (i >> 7)) * NY + ((i >> 3) & 3)
    to_smem = pltpu.make_async_copy(slots_v, slots, s_sem)
    to_smem.start()
    to_smem.wait()
    from_other_core(0)

    def planned(i, plan):
        for number, takes in enumerate(plan):
            if takes:

                @pl.when(i == number)
                def _(takes=takes):
                    for take, t, *groups in takes:
                        for group in groups:
                            take(t, jnp.int32(group))

    def score_group(g):
        zz = from_z(g)
        wait(qbuf.at[pl.ds(zz * NY, NY)], a_recv.at[3, g])
        for yy in range(NY):
            score(zz, yy)

    def score_step(g, _):
        planned(
            g,
            (
                ((take_own, 1, 5), (take_sides, 1, 3), (take_far, 1, 1)),
                ((take_own, 1, 6), (take_sides, 1, 4), (take_far, 1, 2)),
                ((take_own, 1, 7), (take_sides, 1, 5), (take_far, 1, 3)),
                ((take_own, 2, 1), (take_sides, 1, 6), (take_far, 1, 4)),
                ((take_own, 2, 2), (take_sides, 1, 7), (take_far, 1, 5)),
            ),
        )
        score_group(g)
        return 0

    lax.fori_loop(0, 5, score_step, 0)
    take_own(2, 3)
    take_far(1, 6)
    take_own(2, 4)
    take_far(1, 7)
    from_other_core(1)

    def low_step(i, _):
        planned(
            i,
            (
                ((take_sides, 2, 1), (take_own, 2, 5)),
                ((take_sides, 2, 2), (take_own, 2, 6, 7)),
                ((take_sides, 2, 3),),
                ((take_sides, 2, 4), (take_far, 2, 1)),
                ((take_sides, 2, 5),),
                ((take_sides, 2, 6), (take_far, 2, 2)),
                ((take_sides, 2, 7), (take_far, 2, 3)),
                ((take_far, 2, 4),),
            ),
        )
        g = jnp.where(i < 4, i + 3, jnp.where(i == 4, 1, jnp.where(i == 5, 7, jnp.where(i == 6, 2, 0))))

        @pl.when((i == 2) | (i == 3) | (i == 5))
        def _():
            score_group(g)

        mix_group(0, g)
        return 0

    lax.fori_loop(0, NZ, low_step, 0)
    step(3, (take_far, 2, 5))
    from_other_core(2)

    lax.fori_loop(0, NZ, lambda i, _: (mix_group(1, far_first(i)), 0)[1], 0)

    def unpack(i, _):
        g = far_first(i)
        zz = (z + dz_of(g)) % NZ
        for half in range(2):
            wait(landed.at[half, pl.ds(zz * NY, NY)], o_recv.at[half, g])
        for yy in range(NY):
            n = zz * NY + yy
            lo, hi = landed[0, n].astype(jnp.float32), landed[1, n].astype(jnp.float32)
            obuf[n, 0:HALF] = jnp.where(low_lanes, lo, pltpu.roll(hi, HALF, 1)).astype(jnp.bfloat16)
            obuf[n, HALF:BLOCK] = jnp.where(low_lanes, pltpu.roll(lo, HALF, 1), hi).astype(jnp.bfloat16)
            columns = pl.ds(pl.multiple_of((yy * NZ + zz) * BLOCK, BLOCK), BLOCK)
            pltpu.make_async_copy(obuf.at[n], out_hbm.at[:, columns], f_sem).start()
        return 0

    lax.fori_loop(0, NZ, unpack, 0)

    for t in range(4):
        wait(kv[t % 3].at[pl.ds(0, NY * NZ - 1)], a_send.at[t])
    for i in range(3):
        wait(kbuf.at[pl.ds(0, 2 * NZ * NY)], x_send.at[i])
    wait(kbuf, c_send)
    wait(lists_v.at[0], l_send)

    @pl.when(z_lo != c)
    def _():
        wait(lists_v.at[0], l_send)

    for half in range(2):
        wait(mixed.at[half, pl.ds(0, NY * NZ - 1)], o_send.at[half])
    wait(out_hbm, f_sem)


def on_device(query_rows, key_rows, value_rows, block_lists):
    dma = pltpu.SemaphoreType.DMA
    return pl.pallas_call(
        kernel,
        out_shape=jax.ShapeDtypeStruct(query_rows.shape, jnp.bfloat16),
        in_specs=[pl.BlockSpec(memory_space=pl.ANY)] * 4,
        out_specs=pl.BlockSpec(memory_space=pl.ANY),
        scratch_shapes=[
            pltpu.VMEM((2 * SLABS, BLOCK, BLOCK), jnp.bfloat16),
            pltpu.VMEM((2 * SLABS, HALF, BLOCK), jnp.bfloat16),
            pltpu.VMEM((2 * SLABS, HALF, BLOCK), jnp.bfloat16),
            pltpu.VMEM((NY * NZ, BLOCK, BLOCK), jnp.bfloat16),
            pltpu.VMEM(value_rows.shape, jnp.bfloat16),
            pltpu.VMEM((NY * NZ, HALF, BLOCK), jnp.bfloat16),
            pltpu.VMEM((NY * NZ, HALF, BLOCK), jnp.bfloat16),
            pltpu.VMEM((NY * NZ, 2 * BLOCK, LIVE * HALF), jnp.bfloat16),
            pltpu.VMEM((NY * NZ, HALF, BLOCK), jnp.float32),
            pltpu.VMEM((2, NY * NZ, HALF, BLOCK), jnp.bfloat16),
            pltpu.VMEM((2, NY * NZ, HALF, BLOCK), jnp.bfloat16),
            pltpu.VMEM((NY * NZ, BLOCK, BLOCK), jnp.bfloat16),
            pltpu.VMEM((2, LIVE, 32), jnp.int32),
            pltpu.VMEM((2, LIVE, 32), jnp.int32),
            pltpu.SMEM((2, LIVE, 32), jnp.int32),
            dma, dma((4,)), dma((NY,)), dma((4, NZ)), dma((3,)), dma((3, NZ)), dma((3, NZ)), dma((3, NZ)), dma, dma((3,)),
            dma, dma, dma, dma((2,)), dma((2, NZ)), dma,
        ],
        compiler_params=pltpu.CompilerParams(collective_id=0, has_side_effects=True, vmem_limit_bytes=52 * 2**20),
        name="attention",
    )(query_rows, key_rows, value_rows, jnp.swapaxes(block_lists, 1, 2))


def solution(mesh):
    in_specs = (P(("blk", "head"), None), P(("blk", "head"), None), P(("blk", "head"), None), P("head", "blk", None))
    return jax.shard_map(
        on_device, mesh=mesh, in_specs=in_specs, out_specs=P(("blk", "head"), None), check_vma=False
    )
```

time: 113 us -> 112 us (level)
    pallas_call x1, Pallas kernels: 111 us -> 110 us  [on_device(): pl.pallas_call(kernel, out_shape=jax.ShapeDtypeStruct(query_rows.shape, j...]
where the time goes in v3:
time: 112 us; the launch traced here: 111 us
  Pallas kernels  110 us (98%)
  local copies, waits for them, and re-layouts  1.67 us (1%)
    pallas_call x1, Pallas kernels, on_device(): pl.pallas_call(kernel, out_shape=jax.ShapeDtypeStruct(query_rows.shape, j...  110 us

profile of v3, /device:TPU:1, one launch (start us, length us, event | category | flops | bytes accessed | tf_op | source)
XLA Modules:
  0.0 111.5 jit_solution(18426053709308095401)
XLA Ops:
  0.0 0.0 copy-start
  0.0 0.7 copy-done
  0.7 109.8 %attention.1 = bf16[128,4096]{1,0:T(8,128)(2,1)S(1)} custom-call(bf16[128,4096]{1,0:T(8,128)(2,1)} %q_hbm.1, bf16[128,4096]{1,0:T(8,128)(2,1)} %k_hbm.1, bf16[128,4096]{1,0:T(8,128)(2,1)} %v_hbm.1, s32[1,16,32]{2,1,0:T(8,128)S(1)} %bitcast.1), custom_call_target="tpu_custom_call" | custom-call | tf_op jit(solution)/shard_map/attention/pallas_call | solution.py:372
  110.5 1.0 copy.6
Async XLA Ops:
  0.0 0.7 copy-start

commit v4 on v3

--- a/solution.py
+++ b/solution.py
@@ -40,10 +40,10 @@
 
 
 def kernel(
-    q_hbm, k_hbm, v_hbm, lists_hbm, out_hbm,
-    kbuf, lobuf, hibuf, qbuf, vraw, lo_out, hi_out, weights, totals, mixed, landed, obuf, lists_v, slots_v, slots,
+    q_hbm, k_hbm, v_hbm, lists_hbm, out_ref,
+    kbuf, lobuf, hibuf, qbuf, vraw, lo_out, hi_out, weights, totals, mixed, landed, lists_v, slots_v, slots,
     v_sem, a_send, near_recv, a_recv, x_send, left_recv, right_recv, far_recv, c_send, c_recv,
-    l_send, l_recv, s_sem, o_send, o_recv, f_sem,
+    l_send, l_recv, s_sem, o_send, o_recv,
 ):
     blk, head = lax.axis_index("blk"), lax.axis_index("head")
     x, z_lo = blk % NX, blk // NX
@@ -82,8 +82,6 @@
         hi_out[h] = jnp.where(low_lanes, pltpu.roll(top, HALF, 1), bottom).astype(jnp.bfloat16)
         return 0
 
-    load_v.wait()
-    lax.fori_loop(0, NY * NZ // 2, lambda i, _: pack(2 * i + 1, pack(2 * i, 0)), 0)
     pl.semaphore_wait(barrier, NY * NZ - 1 + 4)
 
     def target(t, zz, yy):
@@ -204,9 +202,12 @@
                 pltpu.make_async_copy(src, place, o_recv.at[half, g]).start()
 
     to_both(piece(0, z, y), kbuf.at[slab(x, z) + y], 0, 0)
-    for t in range(3):
-        send_near(t)
-    send_all(0, 1, (0,))
+    send_near(0)
+    send_all(0, 1, (0, 1, 3, 2))
+    load_v.wait()
+    lax.fori_loop(0, NY * NZ // 2, lambda i, _: pack(2 * i + 1, pack(2 * i, 0)), 0)
+    send_near(1)
+    send_near(2)
 
     owner_z = z_hi * 2 + c
     remote(lists_hbm.at[0], lists_v.at[z_lo], l_send, l_recv, device(x, y, owner_z, 1 - c))
@@ -229,26 +230,17 @@
 
     gather_near_block(1)
     gather_near_block(3)
-    send(0, 1, (1, 3, 2))
-    send(0, 2, (1, 3, 2))
     gather_near_block(2)
     swap_own_plane()
     take_own(1, 0)
-    send(0, 3, (1, 3, 2))
-    send(0, 4, (1, 3, 2))
-    take_own(2, 0)
-    send(0, 5, (1, 3, 2))
-    send(0, 6, (1, 3, 2))
     take_own(0, 1)
     take_sides(0, 0)
-    send(0, 7, (1, 3, 2))
     send_all(1, 1, (0, 1, 3, 2))
     take_own(0, 2)
     take_sides(1, 0)
     send_near(3)
     lax.fori_loop(1, 5, lambda g, _: (send(3, g, (0, 1, 3, 2)), 0)[1], 0)
     take_own(0, 3)
-    take_sides(2, 0)
     take_far(0, 0)
     send_all(2, 1, (0, 1, 3, 2))
     send_all(3, 5, (0, 1, 3, 2))
@@ -256,7 +248,6 @@
     take_sides(0, 1)
     take_far(1, 0)
     take_sides(0, 2)
-    take_far(2, 0)
     step(3, (take_own, 0, 5), (take_sides, 0, 3), (take_far, 0, 1))
     step(2, (take_own, 1, 1), (take_sides, 0, 6), (take_far, 0, 4))
     step(2, (take_own, 1, 3), (take_sides, 1, 1), (take_far, 0, 6))
@@ -291,7 +282,7 @@
             (
                 ((take_own, 1, 5), (take_sides, 1, 3), (take_far, 1, 1)),
                 ((take_own, 1, 6), (take_sides, 1, 4), (take_far, 1, 2)),
-                ((take_own, 1, 7), (take_sides, 1, 5), (take_far, 1, 3)),
+                ((take_own, 1, 7), (take_sides, 1, 5), (take_own, 2, 0), (take_far, 1, 3)),
                 ((take_own, 2, 1), (take_sides, 1, 6), (take_far, 1, 4)),
                 ((take_own, 2, 2), (take_sides, 1, 7), (take_far, 1, 5)),
             ),
@@ -302,6 +293,7 @@
     lax.fori_loop(0, 5, score_step, 0)
     take_own(2, 3)
     take_far(1, 6)
+    take_sides(2, 0)
     take_own(2, 4)
     take_far(1, 7)
     from_other_core(1)
@@ -313,7 +305,7 @@
                 ((take_sides, 2, 1), (take_own, 2, 5)),
                 ((take_sides, 2, 2), (take_own, 2, 6, 7)),
                 ((take_sides, 2, 3),),
-                ((take_sides, 2, 4), (take_far, 2, 1)),
+                ((take_sides, 2, 4), (take_far, 2, 0, 1)),
                 ((take_sides, 2, 5),),
                 ((take_sides, 2, 6), (take_far, 2, 2)),
                 ((take_sides, 2, 7), (take_far, 2, 3)),
@@ -343,10 +335,9 @@
         for yy in range(NY):
             n = zz * NY + yy
             lo, hi = landed[0, n].astype(jnp.float32), landed[1, n].astype(jnp.float32)
-            obuf[n, 0:HALF] = jnp.where(low_lanes, lo, pltpu.roll(hi, HALF, 1)).astype(jnp.bfloat16)
-            obuf[n, HALF:BLOCK] = jnp.where(low_lanes, pltpu.roll(lo, HALF, 1), hi).astype(jnp.bfloat16)
             columns = pl.ds(pl.multiple_of((yy * NZ + zz) * BLOCK, BLOCK), BLOCK)
-            pltpu.make_async_copy(obuf.at[n], out_hbm.at[:, columns], f_sem).start()
+            out_ref[0:HALF, columns] = jnp.where(low_lanes, lo, pltpu.roll(hi, HALF, 1)).astype(jnp.bfloat16)
+            out_ref[HALF:BLOCK, columns] = jnp.where(low_lanes, pltpu.roll(lo, HALF, 1), hi).astype(jnp.bfloat16)
         return 0
 
     lax.fori_loop(0, NZ, unpack, 0)
@@ -364,7 +355,6 @@
 
     for half in range(2):
         wait(mixed.at[half, pl.ds(0, NY * NZ - 1)], o_send.at[half])
-    wait(out_hbm, f_sem)
 
 
 def on_device(query_rows, key_rows, value_rows, block_lists):
@@ -373,7 +363,7 @@
         kernel,
         out_shape=jax.ShapeDtypeStruct(query_rows.shape, jnp.bfloat16),
         in_specs=[pl.BlockSpec(memory_space=pl.ANY)] * 4,
-        out_specs=pl.BlockSpec(memory_space=pl.ANY),
+        out_specs=pl.BlockSpec(memory_space=pltpu.VMEM),
         scratch_shapes=[
             pltpu.VMEM((2 * SLABS, BLOCK, BLOCK), jnp.bfloat16),
             pltpu.VMEM((2 * SLABS, HALF, BLOCK), jnp.bfloat16),
@@ -386,12 +376,11 @@
             pltpu.VMEM((NY * NZ, HALF, BLOCK), jnp.float32),
             pltpu.VMEM((2, NY * NZ, HALF, BLOCK), jnp.bfloat16),
             pltpu.VMEM((2, NY * NZ, HALF, BLOCK), jnp.bfloat16),
-            pltpu.VMEM((NY * NZ, BLOCK, BLOCK), jnp.bfloat16),
             pltpu.VMEM((2, LIVE, 32), jnp.int32),
             pltpu.VMEM((2, LIVE, 32), jnp.int32),
             pltpu.SMEM((2, LIVE, 32), jnp.int32),
             dma, dma((4,)), dma((NY,)), dma((4, NZ)), dma((3,)), dma((3, NZ)), dma((3, NZ)), dma((3, NZ)), dma, dma((3,)),
-            dma, dma, dma, dma((2,)), dma((2, NZ)), dma,
+            dma, dma, dma, dma((2,)), dma((2, NZ)),
         ],
         compiler_params=pltpu.CompilerParams(collective_id=0, has_side_effects=True, vmem_limit_bytes=52 * 2**20),
         name="attention",

time: 112 us -> 110 us (0.982)
    pallas_call x1, Pallas kernels: 110 us -> 109 us  [on_device(): pl.pallas_call(kernel, out_shape=jax.ShapeDtypeStruct(query_rows.shape, j...]
where the time goes in v4:
time: 110 us
  Pallas kernels  109 us (99%)
  local copies, waits for them, and re-layouts  1.67 us (2%)
    pallas_call x1, Pallas kernels, on_device(): pl.pallas_call(kernel, out_shape=jax.ShapeDtypeStruct(query_rows.shape, j...  109 us

profile of v4, /device:TPU:1, one launch (start us, length us, event | category | flops | bytes accessed | tf_op | source)
XLA Modules:
  0.0 110.3 jit_solution(10578277473877076178)
XLA Ops:
  0.0 0.0 copy-start
  0.0 0.7 copy-done
  0.7 108.6 %attention.1 = bf16[128,4096]{1,0:T(8,128)(2,1)S(1)} custom-call(bf16[128,4096]{1,0:T(8,128)(2,1)} %q_hbm.1, bf16[128,4096]{1,0:T(8,128)(2,1)} %k_hbm.1, bf16[128,4096]{1,0:T(8,128)(2,1)} %v_hbm.1, s32[1,16,32]{2,1,0:T(8,128)S(1)} %bitcast.1), custom_call_target="tpu_custom_call" | custom-call | tf_op jit(solution)/shard_map/attention/pallas_call | solution.py:362
  109.3 1.0 copy.6
Async XLA Ops:
  0.0 0.7 copy-start

commit v5 on v4

--- a/solution.py
+++ b/solution.py
@@ -66,8 +66,8 @@
     def greet(to):
         pl.semaphore_signal(barrier, inc=1, device_id=to, device_id_type=MESH)
 
-    for dy in range(NY):
-        for dz in range(NZ):
+    for dz in (4, 3, 5, 2, 6, 1, 7, 0):
+        for dy in (2, 1, 3, 0):
             if dy or dz:
                 greet(device(x, (y + dy) % NY, (z + dz) % NZ, c))
     greet(right)

time: 110 us -> 111 us (level)
  no operation moved by 1% of the time
where the time goes in v5:
time: 111 us; the launch traced here: 110 us
  Pallas kernels  109 us (98%)
  local copies, waits for them, and re-layouts  1.67 us (2%)
    pallas_call x1, Pallas kernels, on_device(): pl.pallas_call(kernel, out_shape=jax.ShapeDtypeStruct(query_rows.shape, j...  109 us

profile of v5, /device:TPU:1, one launch (start us, length us, event | category | flops | bytes accessed | tf_op | source)
XLA Modules:
  0.0 110.4 jit_solution(12422106662842138829)
XLA Ops:
  0.0 0.0 copy-start
  0.0 0.7 copy-done
  0.7 108.7 %attention.1 = bf16[128,4096]{1,0:T(8,128)(2,1)S(1)} custom-call(bf16[128,4096]{1,0:T(8,128)(2,1)} %q_hbm.1, bf16[128,4096]{1,0:T(8,128)(2,1)} %k_hbm.1, bf16[128,4096]{1,0:T(8,128)(2,1)} %v_hbm.1, s32[1,16,32]{2,1,0:T(8,128)S(1)} %bitcast.1), custom_call_target="tpu_custom_call" | custom-call | tf_op jit(solution)/shard_map/attention/pallas_call | solution.py:362
  109.4 1.0 copy.6
Async XLA Ops:
  0.0 0.7 copy-start
